TPU v7x, 1024 devices: a whole 4x4x32 slice. The times are simulated.
1024 devices in a mesh: lon: 16 (over x, y), lat: 16 (over z_lo), comp: 4 (over z_hi, core).
Axes of the slice: x: 4, y: 4, z: 32 (z_hi: 2, z_lo: 16; z = z_hi * 16 + z_lo), core: 2. Of those that a mesh axis runs over, the one named last changes fastest.
Arguments:
- fields: float32 [4, 8, 768, 8192], P('comp', None, 'lat', 'lon'), may hold values from -6 to 6
- diffusion: float32 [4, 768, 8192], P('comp', 'lat', 'lon'), may hold values from 0.04 to 0.24
- exchange_coef: float32 [4, 768, 8192], P('comp', 'lat', 'lon'), may hold values from 0.2 to 1
- sea_seen: bfloat16 [768, 8192], P('lat', 'lon'), may hold values from -6 to 6
- remap_code: int32 [8, 768, 8192], P(None, 'lat', 'lon'), may hold values from 0 to 47
- remap_weight: float32 [8, 768, 8192], P(None, 'lat', 'lon'), may hold values from 0.05 to 0.25
- land_sea: int32 [768, 8192], P('lat', 'lon'), may hold values 0 or 1
- fold_partner: int32 [8192], replicated, may hold values from 0 to 8191, as said below
Outputs:
- updated: float32 [4, 8, 768, 8192], P('comp', None, 'lat', 'lon')
- contrast: float32 [4, 768, 8192], P('comp', 'lat', 'lon')
Inputs may be any that keep to these rules, and one draw needn't show every extreme that they name: fold_partner[j] = (s - j) mod 8192 for one whole number s.
All inputs are finite; a program needn't handle non-finite values. No bound on the sum of `land_sea` on one device may be relied on, other than what follows from the above.
Results may differ from a plain program's by a relative error of at most 0.0021.
Values may be sent and summed in bfloat16 or wider, within the bound.
A program may use at most 32 MiB of HBM per device.

v0:
```python
import jax
import jax.numpy as jnp
from jax import lax
from jax.sharding import PartitionSpec as P

SUBSTEPS = 2
WIN = 4


air_gain = 0.5


def extended(shard, sides, width):
    for axis, dim in sides:
        size, length = (lax.axis_size(axis), shard.shape[dim])
        up = [(i, (i + 1) % size) for i in range(size)]
        down = [(j, i) for i, j in up]
        last = lax.slice_in_dim(shard, length - width, length, axis=dim)
        leading = lax.slice_in_dim(shard, 0, width, axis=dim)
        before = lax.ppermute(last, axis, up)
        after = lax.ppermute(leading, axis, down)
        shard = jnp.concatenate([before, shard, after], axis=dim)
    return shard


def broadcast(shard, axis, root):
    mine = lax.axis_index(axis) == root
    return lax.psum(jnp.where(mine, shard, jnp.zeros_like(shard)), axis)


def window_slices(flux_tile):
    row_count, col_count = flux_tile.shape
    padded = jnp.pad(flux_tile, ((1, WIN - 2), (1, WIN - 2)), mode="edge")
    return [
        padded[row_shift : row_shift + row_count, col_shift : col_shift + col_count]
        for row_shift in range(WIN)
        for col_shift in range(WIN)
    ]


def remap_sum(slices, remap_code, remap_weight, first_code):
    total = jnp.zeros(remap_weight.shape[1:], jnp.float32)
    for offset, tile in enumerate(slices):
        chosen = jnp.sum(jnp.where(remap_code == first_code + offset, remap_weight, 0.0), axis=0)
        total = total + chosen * tile.astype(jnp.float32)
    return total


def fold_cols(whole_rows, start, width):
    reversed_rows = whole_rows[..., ::-1]
    doubled = jnp.concatenate([reversed_rows, reversed_rows], axis=-1)
    return lax.dynamic_slice_in_dim(doubled, start, width, axis=doubled.ndim - 1)


def substep_apply(current, diffusion_tile, fold_partner, is_ocean):
    padded = extended(current, (("lon", 2), ("lat", 1)), 1)
    lat_index = lax.axis_index("lat")
    lat_count = lax.axis_size("lat")
    col_count = current.shape[2]
    whole_top = lax.all_gather(current[:, -1:, :], "lon", axis=2, tiled=True)
    total_cols = whole_top.shape[2]
    fold_start = jnp.mod(
        lax.axis_index("lon") * col_count + total_cols - 1 - fold_partner[0], total_cols
    )
    fold_row = fold_cols(whole_top[:, 0, :], fold_start, col_count)
    above_row = jnp.where(
        lat_index == lat_count - 1, jnp.where(is_ocean, fold_row, 0.0), padded[:, -1, 1:-1]
    )
    below_row = jnp.where(lat_index == 0, 0.0, padded[:, 0, 1:-1])
    north_side = jnp.concatenate([padded[:, 2:-1, 1:-1], above_row[:, None, :]], axis=1)
    south_side = jnp.concatenate([below_row[:, None, :], padded[:, 1:-2, 1:-1]], axis=1)
    east_side = padded[:, 1:-1, 2:]
    west_side = padded[:, 1:-1, :-2]
    return current + diffusion_tile * (
        north_side + south_side + east_side + west_side - 4.0 * current
    )


def shards(
    fields, diffusion, exchange_coef, sea_seen, remap_code, remap_weight, land_sea, fold_partner
):
    member_index = lax.axis_index("comp")
    member_count = lax.axis_size("comp") - 1
    is_ocean = member_index == member_count
    current = fields[0]
    for substep in range(SUBSTEPS):
        current = substep_apply(current, diffusion[0], fold_partner, is_ocean)
    sea_prior = sea_seen.astype(jnp.float32)
    lowest = current[0]
    air_flux = jnp.where(is_ocean, 0.0, exchange_coef[0] * (sea_prior - lowest)).astype(
        jnp.bfloat16
    )
    member_tiles = lax.all_gather(air_flux[None], "comp", axis=0, tiled=True)
    all_slices = []
    for member in range(member_count):
        all_slices = all_slices + window_slices(member_tiles[member])
    ocean_flux = remap_sum(all_slices, remap_code, remap_weight, 0) / member_count
    ocean_flux = ocean_flux * land_sea.astype(jnp.float32)
    surface = jnp.where(
        is_ocean, lowest + ocean_flux, lowest + air_gain * air_flux.astype(jnp.float32)
    )
    updated = jnp.concatenate([surface[None], current[1:]], axis=0)
    sea_new = broadcast(surface.astype(jnp.bfloat16), "comp", member_count).astype(jnp.float32)
    contrast = sea_new - jnp.where(is_ocean, sea_prior, surface)
    return (updated[None], contrast[None])


def solution(mesh):
    placed = (
        P("comp", None, "lat", "lon"),
        P("comp", "lat", "lon"),
        P("comp", "lat", "lon"),
        P("lat", "lon"),
        P(None, "lat", "lon"),
        P(None, "lat", "lon"),
        P("lat", "lon"),
        P(),
    )
    return jax.shard_map(
        shards,
        mesh=mesh,
        in_specs=placed,
        out_specs=(P("comp", None, "lat", "lon"), P("comp", "lat", "lon")),
        check_vma=False,
    )
```

profile of v0, /device:TPU:2, one launch (start us, length us, event | category | flops | bytes accessed | tf_op | source)
XLA Modules:
  0.0 263.8 jit_solution(6338460365469380394)
XLA Ops:
  0.6 1.7 copy.80
  2.4 3.6 %collective-permute-start = (f32[8,48,1]{2,0,1:T(8,128)S(1)}, f32[8,48,1]{2,0,1:T(8,128)S(1)}, u32[]{:S(2)}, u32[]{:S(2)}) collective-permute-start(f32[8,48,1]{2,0,1:T(8,128)S(1)} %get-tuple-element.66), channel_id=1, source_target_pairs={{0,64},{64,128},{128,192},{192,256},{256,320},{320,384},{384,448},... | collective-permute-start | bytes 4616 | tf_op jit(solution)/shard_map/ppermute | solution.py:20
  6.1 4.5 %collective-permute-start.1 = (f32[8,48,1]{2,0,1:T(8,128)S(1)}, f32[8,48,1]{2,0,1:T(8,128)S(1)}, u32[]{:S(2)}, u32[]{:S(2)}) collective-permute-start(f32[8,48,1]{2,0,1:T(8,128)S(1)} %get-tuple-element.65), channel_id=1, source_target_pairs={{64,0},{128,64},{192,128},{256,192},{320,256},{384,320},{448,384},... | collective-permute-start | bytes 4616 | tf_op jit(solution)/shard_map/ppermute | solution.py:21
  10.6 6.8 %select_reduce_fusion.47 = (f32[48,512]{1,0:T(8,128)S(1)}, f32[48,512]{1,0:T(8,128)}, f32[48,512]{1,0:T(8,128)}, f32[48,512]{1,0:T(8,128)}, f32[48,512]{1,0:T(8,...) fusion(f32[8,48,512]{2,1,0:T(8,128)S(1)} %copy-done.1, ...), kind=kLoop, calls=%fused_computation.66 | loop fusion | flops 27131904 | bytes 6291456 | tf_op jit(solution)/shard_map/reduce_sum | solution.py:44
  17.7 3.8 %collective-permute-start.3 = (f32[8,1,514]{2,0,1:T(8,128)S(1)}, f32[8,1,514]{2,0,1:T(8,128)S(1)}, u32[]{:S(2)}, u32[]{:S(2)}) collective-permute-start(f32[8,1,514]{2,0,1:T(8,128)S(1)} %get-tuple-element.57), channel_id=1, source_target_pairs={{0,4},{4,8},{8,12},{12,16},{16,20},{20,24},{24,28},{28,32},{32,36}... | collective-permute-start | bytes 49352 | tf_op jit(solution)/shard_map/ppermute | solution.py:20
  21.5 33.2 %all_gather.9 = f32[8,1,8192]{2,0,1:T(8,128)S(1)} all-gather(f32[8,1,512]{2,0,1:T(8,128)S(1)} %slice.452), channel_id=1, replica_groups=mesh['lon'=16,'lat'=16,'comp'=4] {'lon'}, dimensions={2}, use_global_device_ids=true | all-gather | bytes 278528 | tf_op jit(solution)/shard_map/all_gather | solution.py:60
  54.7 1.3 slice.356
  56.7 4.5 %rev.6 = f32[8,8192]{1,0:T(8,128)S(1)} reverse(f32[8,8192]{1,0:T(8,128)S(1)} %bitcast.56), dimensions={1} | reverse | bytes 524288 | tf_op jit(solution)/shard_map/rev | solution.py:50
  61.1 20.1 %collective-permute-start.2 = (f32[8,1,514]{2,0,1:T(8,128)S(1)}, f32[8,1,514]{2,0,1:T(8,128)S(1)}, u32[]{:S(2)}, u32[]{:S(2)}) collective-permute-start(f32[8,1,514]{2,0,1:T(8,128)S(1)} %get-tuple-element.58), channel_id=1, source_target_pairs={{4,0},{8,4},{12,8},{16,12},{20,16},{24,20},{28,24},{32,28},{36,32}... | collective-permute-start | bytes 49352 | tf_op jit(solution)/shard_map/ppermute | solution.py:21
  81.4 1.4 collective-permute-done.2
  84.6 1.9 collective-permute-start.4
  86.6 6.0 %collective-permute-start.5 = (f32[8,48,1]{2,1,0:T(8,128)S(1)}, f32[8,48,1]{2,1,0:T(8,128)S(1)}, u32[]{:S(2)}, u32[]{:S(2)}) collective-permute-start(f32[8,48,1]{2,1,0:T(8,128)S(1)} %get-tuple-element.61), channel_id=1, source_target_pairs={{64,0},{128,64},{192,128},{256,192},{320,256},{384,320},{448,384},... | collective-permute-start | bytes 4616 | tf_op jit(solution)/shard_map/ppermute | solution.py:21
  92.8 1.5 collective-permute-done.4
  94.3 1.5 collective-permute-done.5
  96.0 20.5 %collective-permute-start.6 = (f32[8,1,514]{2,1,0:T(1,128)S(1)}, f32[8,1,514]{2,1,0:T(1,128)S(1)}, u32[]{:S(2)}, u32[]{:S(2)}) collective-permute-start(f32[8,1,514]{2,1,0:T(1,128)S(1)} %get-tuple-element.56), channel_id=1, source_target_pairs={{4,0},{8,4},{12,8},{16,12},{20,16},{24,20},{28,24},{32,28},{36,32}... | collective-permute-start | bytes 49352 | tf_op jit(solution)/shard_map/ppermute | solution.py:21
  116.4 25.1 %all_gather.10 = f32[8,1,8192]{2,0,1:T(8,128)S(1)} all-gather(f32[8,1,512]{2,0,1:T(8,128)S(1)} %copy.28), channel_id=1, replica_groups=mesh['lon'=16,'lat'=16,'comp'=4] {'lon'}, dimensions={2}, use_global_device_ids=true | all-gather | bytes 278528 | tf_op jit(solution)/shard_map/all_gather | solution.py:60
  141.6 4.5 %rev.7 = f32[8,8192]{1,0:T(8,128)S(1)} reverse(f32[8,8192]{1,0:T(8,128)S(1)} %bitcast.57), dimensions={1} | reverse | bytes 524288 | tf_op jit(solution)/shard_map/rev | solution.py:50
  146.0 1.9 collective-permute-start.7
  148.2 19.7 %collective-permute-done.7 = f32[8,1,514]{2,1,0:T(1,128)S(1)} collective-permute-done((f32[8,1,514]{2,1,0:T(1,128)S(1)}, f32[8,1,514]{2,1,0:T(1,128)S(1)}, u32[]{:S(2)}, u32[]{:S(2)}) %collective-permute-start.7) | collective-permute-done | bytes 16480 | tf_op jit(solution)/shard_map/ppermute | solution.py:20
  169.0 24.3 %all-gather = bf16[192,512]{1,0:T(8,128)(2,1)S(1)} all-gather(bf16[48,512]{1,0:T(8,128)(2,1)S(1)} %fusion.20), channel_id=2, replica_groups=mesh['lon'=16,'lat'=16,'comp'=4] {'comp'}, dimensions={0}, use_global_device_ids=true | all-gather | bytes 245760 | tf_op jit(solution)/shard_map/all_gather | solution.py:93
  195.8 2.7 %convert_select_fusion.1 = (bf16[48,512]{1,0:T(8,128)(2,1)}, f32[48,512]{1,0:T(8,128)S(1)}) fusion(pred[]{:T(512)S(6)} %eq.303, bf16[48,512]{1,0:T(8,128)(2,1)S(1)} %fusion.20, s32[48,512]{1,0:T(8,128)} %param.14, f32[48,512]{1,0:T(8,128)} %get-tuple-element.48, bf16[51,514]{1,0:T(8,128)(2,1)S(1)} %pad_maximum_fusion.6, f32[48,512]{1,0:T(8,128)} %get-tuple-element.49, ...), kind=kLoop, calls=%fused_computation.117 | loop fusion | flops 4423680 | bytes 7037953 | tf_op jit(solution)/shard_map/jit(_where)/select_n | solution.py:28
  198.5 63.6 %psum.7 = bf16[48,512]{1,0:T(8,128)(2,1)S(1)} all-reduce(bf16[48,512]{1,0:T(8,128)(2,1)} %get-tuple-element.53), channel_id=1, replica_groups=mesh['lon'=16,'lat'=16,'comp'=4] {'comp'}, use_global_device_ids=true, to_apply=%region_48.49 | all-reduce | flops 24576 | bytes 98304 | tf_op jit(solution)/shard_map/psum | solution.py:28
  262.1 0.7 fusion.22
  262.8 1.0 maximum_bitcast_fusion
  (131 shorter events, 6.0 us)
Async XLA Ops:
  0.6 9.9 %copy-start.2 = (s32[8,48,512]{2,1,0:T(8,128)S(1)}, s32[8,48,512]{2,1,0:T(8,128)}, u32[]{:S(2)}) copy-start(s32[8,48,512]{2,1,0:T(8,128)} %param.12) | copy-start | bytes 2359300
  2.3 8.2 %copy-start.1 = (f32[8,48,512]{2,1,0:T(8,128)S(1)}, f32[8,48,512]{2,1,0:T(8,128)}, u32[]{:S(2)}) copy-start(f32[8,48,512]{2,1,0:T(8,128)} %param.13) | copy-start | bytes 2359300
  2.4 15.2 %collective-permute-start = (f32[8,48,1]{2,0,1:T(8,128)S(1)}, f32[8,48,1]{2,0,1:T(8,128)S(1)}, u32[]{:S(2)}, u32[]{:S(2)}) collective-permute-start(f32[8,48,1]{2,0,1:T(8,128)S(1)} %get-tuple-element.66), channel_id=1, source_target_pairs={{0,64},{64,128},{128,192},{192,256},{256,320},{320,384},{384,448},... | collective-permute-start | bytes 4616 | tf_op jit(solution)/shard_map/ppermute | solution.py:20
  6.1 11.5 %collective-permute-start.1 = (f32[8,48,1]{2,0,1:T(8,128)S(1)}, f32[8,48,1]{2,0,1:T(8,128)S(1)}, u32[]{:S(2)}, u32[]{:S(2)}) collective-permute-start(f32[8,48,1]{2,0,1:T(8,128)S(1)} %get-tuple-element.65), channel_id=1, source_target_pairs={{64,0},{128,64},{192,128},{256,192},{320,256},{384,320},{448,384},... | collective-permute-start | bytes 4616 | tf_op jit(solution)/shard_map/ppermute | solution.py:21
  17.7 63.6 %collective-permute-start.3 = (f32[8,1,514]{2,0,1:T(8,128)S(1)}, f32[8,1,514]{2,0,1:T(8,128)S(1)}, u32[]{:S(2)}, u32[]{:S(2)}) collective-permute-start(f32[8,1,514]{2,0,1:T(8,128)S(1)} %get-tuple-element.57), channel_id=1, source_target_pairs={{0,4},{4,8},{8,12},{12,16},{16,20},{20,24},{24,28},{28,32},{32,36}... | collective-permute-start | bytes 49352 | tf_op jit(solution)/shard_map/ppermute | solution.py:20
  61.1 21.6 %collective-permute-start.2 = (f32[8,1,514]{2,0,1:T(8,128)S(1)}, f32[8,1,514]{2,0,1:T(8,128)S(1)}, u32[]{:S(2)}, u32[]{:S(2)}) collective-permute-start(f32[8,1,514]{2,0,1:T(8,128)S(1)} %get-tuple-element.58), channel_id=1, source_target_pairs={{4,0},{8,4},{12,8},{16,12},{20,16},{24,20},{28,24},{32,28},{36,32}... | collective-permute-start | bytes 49352 | tf_op jit(solution)/shard_map/ppermute | solution.py:21
  84.6 9.7 %collective-permute-start.4 = (f32[8,48,1]{2,1,0:T(8,128)S(1)}, f32[8,48,1]{2,1,0:T(8,128)S(1)}, u32[]{:S(2)}, u32[]{:S(2)}) collective-permute-start(f32[8,48,1]{2,1,0:T(8,128)S(1)} %get-tuple-element.62), channel_id=1, source_target_pairs={{0,64},{64,128},{128,192},{192,256},{256,320},{320,384},{384,448},... | collective-permute-start | bytes 4616 | tf_op jit(solution)/shard_map/ppermute | solution.py:20
  86.6 9.2 %collective-permute-start.5 = (f32[8,48,1]{2,1,0:T(8,128)S(1)}, f32[8,48,1]{2,1,0:T(8,128)S(1)}, u32[]{:S(2)}, u32[]{:S(2)}) collective-permute-start(f32[8,48,1]{2,1,0:T(8,128)S(1)} %get-tuple-element.61), channel_id=1, source_target_pairs={{64,0},{128,64},{192,128},{256,192},{320,256},{384,320},{448,384},... | collective-permute-start | bytes 4616 | tf_op jit(solution)/shard_map/ppermute | solution.py:21
  96.0 52.0 %collective-permute-start.6 = (f32[8,1,514]{2,1,0:T(1,128)S(1)}, f32[8,1,514]{2,1,0:T(1,128)S(1)}, u32[]{:S(2)}, u32[]{:S(2)}) collective-permute-start(f32[8,1,514]{2,1,0:T(1,128)S(1)} %get-tuple-element.56), channel_id=1, source_target_pairs={{4,0},{8,4},{12,8},{16,12},{20,16},{24,20},{28,24},{32,28},{36,32}... | collective-permute-start | bytes 49352 | tf_op jit(solution)/shard_map/ppermute | solution.py:21
  146.0 21.9 %collective-permute-start.7 = (f32[8,1,514]{2,1,0:T(1,128)S(1)}, f32[8,1,514]{2,1,0:T(1,128)S(1)}, u32[]{:S(2)}, u32[]{:S(2)}) collective-permute-start(f32[8,1,514]{2,1,0:T(1,128)S(1)} %get-tuple-element.55), channel_id=1, source_target_pairs={{0,4},{4,8},{8,12},{12,16},{16,20},{20,24},{24,28},{28,32},{32,36}... | collective-permute-start | bytes 49352 | tf_op jit(solution)/shard_map/ppermute | solution.py:20
  168.0 26.7 %copy-start.38 = (f32[48,512]{1,0:T(8,128)S(1)}, f32[48,512]{1,0:T(8,128)}, u32[]{:S(2)}) copy-start(f32[48,512]{1,0:T(8,128)} %get-tuple-element.37) | copy-start | bytes 294916
  168.1 26.7 %copy-start.39 = (f32[48,512]{1,0:T(8,128)S(1)}, f32[48,512]{1,0:T(8,128)}, u32[]{:S(2)}) copy-start(f32[48,512]{1,0:T(8,128)} %get-tuple-element.38) | copy-start | bytes 294916
  168.1 26.7 %copy-start.40 = (f32[48,512]{1,0:T(8,128)S(1)}, f32[48,512]{1,0:T(8,128)}, u32[]{:S(2)}) copy-start(f32[48,512]{1,0:T(8,128)} %get-tuple-element.39) | copy-start | bytes 294916
  168.1 26.7 %copy-start.41 = (f32[48,512]{1,0:T(8,128)S(1)}, f32[48,512]{1,0:T(8,128)}, u32[]{:S(2)}) copy-start(f32[48,512]{1,0:T(8,128)} %get-tuple-element.40) | copy-start | bytes 294916
  168.1 26.7 %copy-start.42 = (f32[48,512]{1,0:T(8,128)S(1)}, f32[48,512]{1,0:T(8,128)}, u32[]{:S(2)}) copy-start(f32[48,512]{1,0:T(8,128)} %get-tuple-element.41) | copy-start | bytes 294916
  168.1 26.7 %copy-start.43 = (f32[48,512]{1,0:T(8,128)S(1)}, f32[48,512]{1,0:T(8,128)}, u32[]{:S(2)}) copy-start(f32[48,512]{1,0:T(8,128)} %get-tuple-element.42) | copy-start | bytes 294916
  168.9 25.9 %copy-start.35 = (f32[48,512]{1,0:T(8,128)S(1)}, f32[48,512]{1,0:T(8,128)}, u32[]{:S(2)}) copy-start(f32[48,512]{1,0:T(8,128)} %get-tuple-element.34) | copy-start | bytes 294916
  169.0 25.9 %copy-start.36 = (f32[48,512]{1,0:T(8,128)S(1)}, f32[48,512]{1,0:T(8,128)}, u32[]{:S(2)}) copy-start(f32[48,512]{1,0:T(8,128)} %get-tuple-element.35) | copy-start | bytes 294916
  169.0 25.9 %copy-start.37 = (f32[48,512]{1,0:T(8,128)S(1)}, f32[48,512]{1,0:T(8,128)}, u32[]{:S(2)}) copy-start(f32[48,512]{1,0:T(8,128)} %get-tuple-element.36) | copy-start | bytes 294916
  169.0 25.9 %copy-start.32 = (f32[48,512]{1,0:T(8,128)S(1)}, f32[48,512]{1,0:T(8,128)}, u32[]{:S(2)}) copy-start(f32[48,512]{1,0:T(8,128)} %get-tuple-element.31) | copy-start | bytes 294916
  169.0 25.9 %copy-start.33 = (f32[48,512]{1,0:T(8,128)S(1)}, f32[48,512]{1,0:T(8,128)}, u32[]{:S(2)}) copy-start(f32[48,512]{1,0:T(8,128)} %get-tuple-element.32) | copy-start | bytes 294916
  169.0 25.9 %copy-start.34 = (f32[48,512]{1,0:T(8,128)S(1)}, f32[48,512]{1,0:T(8,128)}, u32[]{:S(2)}) copy-start(f32[48,512]{1,0:T(8,128)} %get-tuple-element.33) | copy-start | bytes 294916
  193.3 1.6 copy-start.30
  193.3 1.6 copy-start.31
  (30 other events, 33.7 us)
where the time goes:
time: 264 us
  blocking collectives  146 us (55%)
  starting transfers between devices  62.4 us (24%)
  waiting for transfers between devices  24.1 us (9%)
  local copies, waits for them, and re-layouts  14.8 us (6%)
  other arithmetic  14.3 us (5%)
    psum x1, blocking collectives, broadcast(): return lax.psum(jnp.where(mine, shard, jnp.zeros_like(shard)), axis)  63.6 us
    all_gather x2, blocking collectives, substep_apply(): whole_top = lax.all_gather(current[:, -1:, :], 'lon', axis=2, tiled=True)  58.3 us
    ppermute x4, starting transfers between devices, extended(): after = lax.ppermute(leading, axis, down)  51.1 us
    all_gather x1, blocking collectives, shards(): member_tiles = lax.all_gather(air_flux[None], 'comp', axis=0, tiled=True)  24.3 us
    ppermute x4, waiting for transfers between devices, extended(): before = lax.ppermute(last, axis, up)  21.2 us
    ppermute x4, starting transfers between devices, extended(): before = lax.ppermute(last, axis, up)  11.3 us
    rev x2, local copies, waits for them, and re-layouts, fold_cols(): reversed_rows = whole_rows[..., ::-1]  8.94 us
    reduce_sum x1, other arithmetic, remap_sum(): jnp.sum(jnp.where(remap_code == first_code + offset, remap_weight, 0.0),...  6.82 us
  transfers between devices with their start and end apart: 8, of which 4 were waited for; matrix products, arithmetic and copies ran while one was open for 7% of the time, Pallas kernels for 0%

commit v1 on v0

v1 whole, which is shorter than its diff:
```python
import functools

import jax
import jax.numpy as jnp
from jax import lax
from jax.experimental import pallas as pl
from jax.experimental.pallas import tpu as pltpu
from jax.sharding import PartitionSpec as P

MESH = pl.DeviceIdType.MESH
F32, BF16 = jnp.float32, jnp.bfloat16
ROWS, COLS, SLICES, TAPS, WIN = 48, 512, 8, 8, 4
PADR, PADC = 8, 128
EXTR, EXTC = ROWS + 2 * PADR, COLS + 2 * PADC
HALF = COLS // 2
BLOCKS = COLS // PADC
FOLD_ROWS = 24
N_SIDES = 8
AIR_GAIN = 0.5

MID_R, MID_C = pl.ds(PADR, ROWS), pl.ds(PADC, COLS)
LOW_R, HIGH_R = pl.ds(0, PADR), pl.ds(PADR + ROWS, PADR)
LOW_C, HIGH_C = pl.ds(0, PADC), pl.ds(PADC + COLS, PADC)
FIRST_R, LAST_R = pl.ds(PADR, PADR), pl.ds(ROWS, PADR)
FIRST_C, LAST_C = pl.ds(PADC, PADC), pl.ds(COLS, PADC)

SIDES = (
    (0, 1, LAST_R, MID_C, LOW_R, MID_C),
    (0, -1, FIRST_R, MID_C, HIGH_R, MID_C),
    (1, 0, MID_R, LAST_C, MID_R, LOW_C),
    (-1, 0, MID_R, FIRST_C, MID_R, HIGH_C),
    (1, 1, LAST_R, LAST_C, LOW_R, LOW_C),
    (-1, 1, LAST_R, FIRST_C, LOW_R, HIGH_C),
    (1, -1, FIRST_R, LAST_C, HIGH_R, LOW_C),
    (-1, -1, FIRST_R, FIRST_C, HIGH_R, HIGH_C),
)


def roll(value, shift, axis):
    return pltpu.roll(value, shift % value.shape[axis], axis)


def kernel(
    n_lon,
    n_lat,
    fields,
    diffusion,
    exchange,
    sea_seen,
    code,
    weight,
    land,
    fold,
    updated,
    contrast,
    ext,
    mid,
    upd,
    con,
    exch,
    seen,
    codes,
    weights,
    sea_mask,
    chosen,
    padded,
    shifted,
    share,
    share_in,
    part,
    part_in,
    surf,
    fold_out,
    fold_all,
    fold_at,
    load_sem,
    out_sem,
    halo_send,
    halo_recv,
    pair_send,
    pair_recv,
    fold_send,
    fold_recv,
    ready,
):
    lon, lat, comp = (lax.axis_index(a) for a in ("lon", "lat", "comp"))
    core = lax.rem(comp, 2)
    far = comp >= 2
    is_ocean = comp == 3
    folded = jnp.logical_and(is_ocean, lat == n_lat - 1)
    sibling = (lon, lat, comp + 1 - 2 * core)
    partner = (lon, lat, lax.rem(comp + 2, 4))

    def side_target(east, north):
        return (
            lax.rem(lon + east + n_lon, n_lon),
            lax.rem(lat + north + n_lat, n_lat),
            comp,
        )

    def has(north):
        if north == 0:
            return None
        return lat < n_lat - 1 if north > 0 else lat > 0

    def when(condition, action):
        if condition is None:
            action()
        else:
            pl.when(condition)(action)

    def local(src, dst, index):
        return pltpu.make_async_copy(src, dst, load_sem.at[index])

    loads = [
        local(diffusion.at[0], ext.at[0, MID_R, MID_C], 0),
        local(fields.at[0, 0], ext.at[1, MID_R, MID_C], 1),
        local(code, codes, 2),
        local(weight, weights, 3),
        local(sea_seen, seen, 4),
        local(exchange.at[0], exch, 5),
        local(land, sea_mask, 6),
        local(fields.at[0, pl.ds(1, SLICES - 1)], ext.at[pl.ds(2, SLICES - 1), MID_R, MID_C], 7),
    ]
    fold_load = local(fold.at[pl.ds(0, 1024)], fold_at, 8)
    for load in loads:
        load.start()

    barrier = pltpu.get_barrier_semaphore()

    def greet(target):
        pl.semaphore_signal(barrier, inc=1, device_id=target, device_id_type=MESH)

    for east, north, *_ in SIDES:
        when(has(north), functools.partial(greet, side_target(east, north)))
    greet(sibling)
    pl.when(jnp.logical_not(far))(functools.partial(greet, partner))

    @pl.when(folded)
    def _():
        fold_load.start()
        for away in range(1, n_lon):
            greet((lax.rem(lon + away, n_lon), lat, comp))

    @pl.when(lat == 0)
    def _():
        ext[:, 0:PADR, :] = jnp.zeros((SLICES + 1, PADR, EXTC), F32)

    @pl.when(lat == n_lat - 1)
    def _():
        ext[:, PADR + ROWS : EXTR, :] = jnp.zeros((SLICES + 1, PADR, EXTC), F32)

    expected = (
        3
        + 3 * (lat > 0).astype(jnp.int32)
        + 3 * (lat < n_lat - 1).astype(jnp.int32)
        + far.astype(jnp.int32)
        + (n_lon - 1) * folded.astype(jnp.int32)
    )
    pl.semaphore_wait(barrier, expected)

    @pl.when(far)
    def _():
        pl.semaphore_signal(ready, inc=1, device_id=partner, device_id_type=MESH)

    def halo(group, index):
        east, north, src_r, src_c, dst_r, dst_c = SIDES[index]
        if group == 1:
            planes = pl.ds(2, SLICES - 1)
        elif index < 4:
            planes = pl.ds(0, 2)
        else:
            planes = pl.ds(1, 1)
        slot = group * N_SIDES + index
        return pltpu.make_async_remote_copy(
            ext.at[planes, src_r, src_c],
            ext.at[planes, dst_r, dst_c],
            halo_send.at[slot],
            halo_recv.at[slot],
            device_id=side_target(east, north),
            device_id_type=MESH,
        )

    def send_halos(group):
        for index in range(N_SIDES):
            when(has(SIDES[index][1]), halo(group, index).start)

    def await_halos(group):
        for index in range(N_SIDES):
            when(has(-SIDES[index][1]), halo(group, index).wait_recv)

    def await_sent(group):
        for index in range(N_SIDES):
            when(has(SIDES[index][1]), halo(group, index).wait_send)

    loads[0].wait()
    loads[1].wait()
    send_halos(0)
    loads[7].wait()
    send_halos(1)

    def fold_copy(away):
        return pltpu.make_async_remote_copy(
            fold_out,
            fold_all.at[pl.ds(BLOCKS * lon, BLOCKS)],
            fold_send.at[away],
            fold_recv.at[away],
            device_id=(lax.rem(lon + away, n_lon), lat, comp),
            device_id_type=MESH,
        )

    @pl.when(folded)
    def _():
        fold_out[...] = jnp.zeros((BLOCKS, FOLD_ROWS, PADC), F32)
        for block in range(BLOCKS):
            at = PADC + block * PADC
            for plane in range(SLICES):
                tail = ext[plane + 1, ROWS : ROWS + PADR, at : at + PADC]
                fold_out[block, plane : plane + 1, :] = tail[6:7]
                fold_out[block, SLICES + plane : SLICES + plane + 1, :] = tail[7:8]
            tail = ext[0, ROWS : ROWS + PADR, at : at + PADC]
            fold_out[block, 2 * SLICES : 2 * SLICES + 1, :] = tail[7:8]
        fold_all[pl.ds(BLOCKS * lon, BLOCKS)] = fold_out[...]
        for away in range(1, n_lon):
            fold_copy(away).start()

    loads[2].wait()
    loads[3].wait()
    loads[4].wait()
    loads[5].wait()
    loads[6].wait()

    @pl.when(jnp.logical_not(is_ocean))
    def _():
        first = comp * (WIN * WIN)

        def rows_of(step, carry):
            at = pl.multiple_of(step * 8, 8)
            for block in range(BLOCKS):
                cols = slice(block * PADC, (block + 1) * PADC)
                tap_code = [codes[tap, pl.ds(at, 8), cols] - first for tap in range(TAPS)]
                tap_weight = [weights[tap, pl.ds(at, 8), cols] for tap in range(TAPS)]
                for cell in range(WIN * WIN):
                    terms = [jnp.where(c == cell, w, 0.0) for c, w in zip(tap_code, tap_weight)]
                    while len(terms) > 1:
                        terms = [a + b for a, b in zip(terms[::2], terms[1::2])]
                    chosen[cell, pl.ds(at, 8), cols] = terms[0]
            return carry

        lax.fori_loop(0, ROWS // 8, rows_of, 0)

    @pl.when(folded)
    def _():
        for away in range(1, n_lon):
            fold_copy(away).wait_recv()
        fold_load.wait()
        ahead = fold_at[0] + n_lon * COLS - (lon + 1) * COLS
        start = ahead // PADC
        rest = lax.rem(ahead, PADC)
        total = BLOCKS * n_lon
        window = [fold_all[lax.rem(start + i, total)] for i in range(BLOCKS + 2)]
        spots = lax.broadcasted_iota(jnp.int32, (2 * PADC, PADC), 0) + lax.broadcasted_iota(
            jnp.int32, (2 * PADC, PADC), 1
        )
        pick = jnp.where(spots == PADC + rest, 1.0, 0.0).astype(F32)
        for block in range(BLOCKS + 2):
            pair = jnp.concatenate([window[max(BLOCKS - block, 0)], window[BLOCKS + 1 - block]], axis=1)
            mirrored = jnp.dot(
                pair, pick, precision=lax.Precision.HIGHEST, preferred_element_type=F32
            )
            cols = slice(block * PADC, (block + 1) * PADC)
            beyond = PADR + ROWS
            for plane in range(SLICES):
                ext[plane + 1, beyond + 1 : beyond + 2, cols] = mirrored[plane : plane + 1]
                ext[plane + 1, beyond : beyond + 1, cols] = mirrored[
                    SLICES + plane : SLICES + plane + 1
                ]
            ext[0, beyond : beyond + 1, cols] = mirrored[2 * SLICES : 2 * SLICES + 1]

    def first_substep(plane):
        for block in range(EXTR // 8):
            at = block * 8
            here = ext[plane, at : at + 8, :]
            if block < EXTR // 8 - 1:
                north = ext[plane, at + 1 : at + 9, :]
            else:
                north = roll(here, -1, 0)
            if block > 0:
                south = ext[plane, at - 1 : at + 7, :]
            else:
                south = roll(here, 1, 0)
            east, west = roll(here, -1, 1), roll(here, 1, 1)
            rate = ext[0, at : at + 8, :]
            mid[plane - 1, at : at + 8, :] = here + rate * (north + south + east + west - 4.0 * here)

    def second_substep(plane, block):
        at = PADR + block * 8
        whole = mid[plane - 1, at : at + 8, :]
        here = whole[:, PADC : PADC + COLS]
        north = mid[plane - 1, at + 1 : at + 9, PADC : PADC + COLS]
        south = mid[plane - 1, at - 1 : at + 7, PADC : PADC + COLS]
        east = roll(whole, -1, 1)[:, PADC : PADC + COLS]
        west = roll(whole, 1, 1)[:, PADC : PADC + COLS]
        rate = ext[0, at : at + 8, PADC : PADC + COLS]
        return here + rate * (north + south + east + west - 4.0 * here)

    await_halos(0)
    first_substep(1)

    @pl.when(is_ocean)
    def _():
        for block in range(ROWS // 8):
            rows = slice(block * 8, block * 8 + 8)
            lowest = second_substep(1, block)
            share[0, rows, :] = lowest[:, :HALF]
            share[1, rows, :] = lowest[:, HALF:]

    @pl.when(jnp.logical_not(is_ocean))
    def _():
        for block in range(ROWS // 8):
            rows = slice(block * 8, block * 8 + 8)
            lowest = second_substep(1, block)
            flux = exch[rows, :] * (seen[rows, :].astype(F32) - lowest)
            flux = flux.astype(BF16).astype(F32)
            upd[0, rows, :] = lowest + AIR_GAIN * flux
            at = PADR + block * 8
            padded[at : at + 8, PADC : PADC + COLS] = flux
            padded[at : at + 8, :PADC] = jnp.broadcast_to(flux[:, :1], (8, PADC))
            padded[at : at + 8, PADC + COLS :] = jnp.broadcast_to(flux[:, COLS - 1 :], (8, PADC))
        padded[:PADR, :] = jnp.broadcast_to(padded[PADR : PADR + 1, :], (PADR, EXTC))
        end = PADR + ROWS
        padded[end:, :] = jnp.broadcast_to(padded[end - 1 : end, :], (PADR, EXTC))
        for block in range(EXTR // 8):
            at = block * 8
            whole = padded[at : at + 8, :]
            for step in range(WIN):
                shifted[step, at : at + 8, :] = roll(whole, 1 - step, 1)[:, PADC : PADC + COLS]
        for block in range(ROWS // 8):
            rows = slice(block * 8, block * 8 + 8)
            total = None
            for step in range(WIN):
                for up in range(WIN):
                    at = PADR + block * 8 + up - 1
                    term = chosen[WIN * up + step, rows, :] * shifted[step, at : at + 8, :]
                    total = term if total is None else total + term
            total = total * (sea_mask[rows, :].astype(F32) * (1.0 / 3.0))
            share[0, rows, :] = total[:, :HALF]
            share[1, rows, :] = total[:, HALF:]

    def pair_copy(index, src, dst, target):
        return pltpu.make_async_remote_copy(
            src, dst, pair_send.at[index], pair_recv.at[index], device_id=target, device_id_type=MESH
        )

    give = pair_copy(0, share.at[1 - core], share_in, sibling)
    cross = pair_copy(1, part, part_in, partner)
    finish = pair_copy(2, surf.at[core], surf.at[core], sibling)
    give.start()
    give.wait_recv()
    part[...] = share[core] + share_in[...]

    pl.when(far)(cross.start)

    await_halos(1)

    def other_slice(plane, carry):
        first_substep(plane)
        for block in range(ROWS // 8):
            upd[plane - 1, block * 8 : block * 8 + 8, :] = second_substep(plane, block)
        return carry

    lax.fori_loop(2, SLICES + 1, other_slice, 0)
    rest_out = pltpu.make_async_copy(
        upd.at[pl.ds(1, SLICES - 1)], updated.at[0, pl.ds(1, SLICES - 1)], out_sem.at[0]
    )
    top_out = pltpu.make_async_copy(upd.at[0], updated.at[0, 0], out_sem.at[1])
    con_out = pltpu.make_async_copy(con, contrast.at[0], out_sem.at[2])
    rest_out.start()

    @pl.when(jnp.logical_not(far))
    def _():
        pl.semaphore_wait(ready, 1)
        cross.start()

    pl.when(jnp.logical_not(is_ocean))(top_out.start)

    cross.wait_recv()
    surf[core] = part[...] + part_in[...]
    finish.start()
    finish.wait_recv()

    for block in range(ROWS // 8):
        rows = slice(block * 8, block * 8 + 8)
        ocean = jnp.concatenate([surf[0, rows, :], surf[1, rows, :]], axis=1)
        sea_new = ocean.astype(BF16).astype(F32)

        @pl.when(is_ocean)
        def _():
            upd[0, rows, :] = ocean
            con[rows, :] = sea_new - seen[rows, :].astype(F32)

        @pl.when(jnp.logical_not(is_ocean))
        def _():
            con[rows, :] = sea_new - upd[0, rows, :]

    con_out.start()
    pl.when(is_ocean)(top_out.start)

    await_sent(0)
    await_sent(1)
    give.wait_send()
    cross.wait_send()
    finish.wait_send()

    @pl.when(folded)
    def _():
        for away in range(1, n_lon):
            fold_copy(away).wait_send()

    rest_out.wait()
    top_out.wait()
    con_out.wait()


def shards(n_lon, n_lat, *args):
    fields = args[0]
    vmem, sems = pltpu.VMEM, pltpu.SemaphoreType.DMA
    return pl.pallas_call(
        functools.partial(kernel, n_lon, n_lat),
        out_shape=(
            jax.ShapeDtypeStruct(fields.shape, F32),
            jax.ShapeDtypeStruct((1, ROWS, COLS), F32),
        ),
        in_specs=[pl.BlockSpec(memory_space=pl.ANY)] * 8,
        out_specs=(pl.BlockSpec(memory_space=pl.ANY),) * 2,
        scratch_shapes=[
            vmem((SLICES + 1, EXTR, EXTC), F32),
            vmem((SLICES, EXTR, EXTC), F32),
            vmem((SLICES, ROWS, COLS), F32),
            vmem((ROWS, COLS), F32),
            vmem((ROWS, COLS), F32),
            vmem((ROWS, COLS), BF16),
            vmem((TAPS, ROWS, COLS), jnp.int32),
            vmem((TAPS, ROWS, COLS), F32),
            vmem((ROWS, COLS), jnp.int32),
            vmem((WIN * WIN, ROWS, COLS), F32),
            vmem((EXTR, EXTC), F32),
            vmem((WIN, EXTR, COLS), F32),
            vmem((2, ROWS, HALF), F32),
            vmem((ROWS, HALF), F32),
            vmem((ROWS, HALF), F32),
            vmem((ROWS, HALF), F32),
            vmem((2, ROWS, HALF), F32),
            vmem((BLOCKS, FOLD_ROWS, PADC), F32),
            vmem((BLOCKS * n_lon, FOLD_ROWS, PADC), F32),
            pltpu.SMEM((1024,), jnp.int32),
            sems((9,)),
            sems((3,)),
            sems((2 * N_SIDES,)),
            sems((2 * N_SIDES,)),
            sems((3,)),
            sems((3,)),
            sems((n_lon,)),
            sems((n_lon,)),
            pltpu.SemaphoreType.REGULAR,
        ],
        compiler_params=pltpu.CompilerParams(
            collective_id=0, has_side_effects=True, vmem_limit_bytes=32 * 2**20
        ),
    )(*args)


def solution(mesh):
    placed = (
        P("comp", None, "lat", "lon"),
        P("comp", "lat", "lon"),
        P("comp", "lat", "lon"),
        P("lat", "lon"),
        P(None, "lat", "lon"),
        P(None, "lat", "lon"),
        P("lat", "lon"),
        P(),
    )
    return jax.shard_map(
        functools.partial(shards, mesh.shape["lon"], mesh.shape["lat"]),
        mesh=mesh,
        in_specs=placed,
        out_specs=(P("comp", None, "lat", "lon"), P("comp", "lat", "lon")),
        check_vma=False,
    )
```

time: 264 us -> 54.9 us (0.21)
  the two profiles are of different devices: /device:TPU:2 before, /device:TPU:481 now
where the time goes in v1:
time: 54.9 us; the launch traced here: 54.4 us
  Pallas kernels  44.6 us (81%)
  local copies, waits for them, and re-layouts  9.15 us (17%)
  between operations  0.66 us (1%)
    pallas_call x1, Pallas kernels, shards(): pl.pallas_call(functools.partial(kernel, n_lon, n_lat), out_shape=(jax.Sh...  44.6 us
    unnamed x18, local copies, waits for them, and re-layouts  9.15 us

profile of v1, /device:TPU:481, one launch (start us, length us, event | category | flops | bytes accessed | tf_op | source)
XLA Modules:
  0.0 54.4 jit_solution(12978960396070367498)
XLA Ops:
  0.6 0.0 copy-start
  0.6 1.1 %copy-done = f32[1,8,48,512]{3,2,1,0:T(8,128)S(1)} copy-done((f32[1,8,48,512]{3,2,1,0:T(8,128)S(1)}, f32[1,8,48,512]{3,2,1,0:T(8,128)}, u32[]{:S(2)}) %copy-start) | copy-done | bytes 786456
  1.8 0.0 copy-start.1
  1.8 1.1 %copy-done.1 = s32[8,48,512]{2,1,0:T(8,128)S(1)} copy-done((s32[8,48,512]{2,1,0:T(8,128)S(1)}, s32[8,48,512]{2,1,0:T(8,128)}, u32[]{:S(2)}) %copy-start.1) | copy-done | bytes 786456
  2.9 0.0 copy-start.2
  2.9 1.1 %copy-done.2 = f32[8,48,512]{2,1,0:T(8,128)S(1)} copy-done((f32[8,48,512]{2,1,0:T(8,128)S(1)}, f32[8,48,512]{2,1,0:T(8,128)}, u32[]{:S(2)}) %copy-start.2) | copy-done | bytes 786456
  4.0 0.0 copy-start.3
  4.0 0.9 %copy-done.3 = f32[1,48,512]{2,1,0:T(8,128)S(1)} copy-done((f32[1,48,512]{2,1,0:T(8,128)S(1)}, f32[1,48,512]{2,1,0:T(8,128)}, u32[]{:S(2)}) %copy-start.3) | copy-done | bytes 98328
  4.9 0.0 copy-start.4
  4.9 0.9 %copy-done.4 = f32[1,48,512]{2,1,0:T(8,128)S(1)} copy-done((f32[1,48,512]{2,1,0:T(8,128)S(1)}, f32[1,48,512]{2,1,0:T(8,128)}, u32[]{:S(2)}) %copy-start.4) | copy-done | bytes 98328
  5.8 0.0 copy-start.5
  5.8 0.9 %copy-done.5 = s32[48,512]{1,0:T(8,128)S(1)} copy-done((s32[48,512]{1,0:T(8,128)S(1)}, s32[48,512]{1,0:T(8,128)}, u32[]{:S(2)}) %copy-start.5) | copy-done | bytes 98328
  6.7 0.0 copy-start.6
  6.7 0.8 %copy-done.6 = bf16[48,512]{1,0:T(8,128)(2,1)S(1)} copy-done((bf16[48,512]{1,0:T(8,128)(2,1)S(1)}, bf16[48,512]{1,0:T(8,128)(2,1)}, u32[]{:S(2)}) %copy-start.6) | copy-done | bytes 49176
  7.5 0.0 copy-start.7
  7.5 0.8 %copy-done.7 = s32[8192]{0:T(1024)S(1)} copy-done((s32[8192]{0:T(1024)S(1)}, s32[8192]{0:T(1024)}, u32[]{:S(2)}) %copy-start.7) | copy-done | bytes 32792
  8.3 44.6 %shard_map.95 = (f32[1,8,48,512]{3,2,1,0:T(8,128)S(1)}, f32[1,48,512]{2,1,0:T(8,128)S(1)}) custom-call(f32[1,8,48,512]{3,2,1,0:T(8,128)S(1)} %copy-done, f32[1,48,512]{2,1,0:T(8,128)S(1)} %copy-done.3, f32[1,48,512]{2,1,0:T(8,128)S(1)} %copy-done.4, bf16[48,512]{1,0:T(8,128)(2,1)S(1)} %copy-done.6, s32[8,48,512]{2,1,0:T(8,128)S(1)} %copy-done.1, ...), custom_call_target="tpu_custom_call" | custom-call | tf_op jit(solution)/shard_map/pallas_call | solution.py:428
  52.9 0.9 %copy.12 = f32[1,8,48,512]{3,2,1,0:T(8,128)} copy(f32[1,8,48,512]{3,2,1,0:T(8,128)S(1)} %get-tuple-element.4) | data formatting | bytes 1572864
  53.7 0.6 %copy.13 = f32[1,48,512]{2,1,0:T(8,128)} copy(f32[1,48,512]{2,1,0:T(8,128)S(1)} %get-tuple-element.5) | data formatting | bytes 196608
Async XLA Ops:
  0.6 1.1 %copy-start = (f32[1,8,48,512]{3,2,1,0:T(8,128)S(1)}, f32[1,8,48,512]{3,2,1,0:T(8,128)}, u32[]{:S(2)}) copy-start(f32[1,8,48,512]{3,2,1,0:T(8,128)} %fields.1) | copy-start | bytes 2359300
  1.8 1.1 %copy-start.1 = (s32[8,48,512]{2,1,0:T(8,128)S(1)}, s32[8,48,512]{2,1,0:T(8,128)}, u32[]{:S(2)}) copy-start(s32[8,48,512]{2,1,0:T(8,128)} %code.1) | copy-start | bytes 2359300
  2.9 1.1 %copy-start.2 = (f32[8,48,512]{2,1,0:T(8,128)S(1)}, f32[8,48,512]{2,1,0:T(8,128)}, u32[]{:S(2)}) copy-start(f32[8,48,512]{2,1,0:T(8,128)} %weight.1) | copy-start | bytes 2359300
  4.0 0.9 %copy-start.3 = (f32[1,48,512]{2,1,0:T(8,128)S(1)}, f32[1,48,512]{2,1,0:T(8,128)}, u32[]{:S(2)}) copy-start(f32[1,48,512]{2,1,0:T(8,128)} %diffusion.1) | copy-start | bytes 294916
  4.9 0.9 %copy-start.4 = (f32[1,48,512]{2,1,0:T(8,128)S(1)}, f32[1,48,512]{2,1,0:T(8,128)}, u32[]{:S(2)}) copy-start(f32[1,48,512]{2,1,0:T(8,128)} %exchange.1) | copy-start | bytes 294916
  5.8 0.9 %copy-start.5 = (s32[48,512]{1,0:T(8,128)S(1)}, s32[48,512]{1,0:T(8,128)}, u32[]{:S(2)}) copy-start(s32[48,512]{1,0:T(8,128)} %land.1) | copy-start | bytes 294916
  6.7 0.8 %copy-start.6 = (bf16[48,512]{1,0:T(8,128)(2,1)S(1)}, bf16[48,512]{1,0:T(8,128)(2,1)}, u32[]{:S(2)}) copy-start(bf16[48,512]{1,0:T(8,128)(2,1)} %sea_seen.1) | copy-start | bytes 147460
  7.5 0.8 %copy-start.7 = (s32[8192]{0:T(1024)S(1)}, s32[8192]{0:T(1024)}, u32[]{:S(2)}) copy-start(s32[8192]{0:T(1024)} %fold.1) | copy-start | bytes 98308

commit v2 on v1

--- a/solution.py
+++ b/solution.py
@@ -14,7 +14,6 @@
 EXTR, EXTC = ROWS + 2 * PADR, COLS + 2 * PADC
 HALF = COLS // 2
 BLOCKS = COLS // PADC
-FOLD_ROWS = 24
 N_SIDES = 8
 AIR_GAIN = 0.5
 
@@ -33,6 +32,12 @@
     (-1, 1, LAST_R, FIRST_C, LOW_R, HIGH_C),
     (1, -1, FIRST_R, LAST_C, HIGH_R, LOW_C),
     (-1, -1, FIRST_R, FIRST_C, HIGH_R, HIGH_C),
+)
+
+
+FOLD_LINES = (
+    ((1, 0, ROWS - 2), (1, 1, ROWS - 1), (0, 2, ROWS - 1)),
+    tuple((plane, 8 * side + plane - 2, ROWS - 2 + side) for side in range(2) for plane in range(2, SLICES + 1)),
 )
 
 
@@ -55,8 +60,6 @@
     contrast,
     ext,
     mid,
-    upd,
-    con,
     exch,
     seen,
     codes,
@@ -70,11 +73,17 @@
     part,
     part_in,
     surf,
-    fold_out,
-    fold_all,
+    edge_out,
+    side_out,
+    rows_out,
+    rows_in,
+    corner_in,
+    fold_out_0,
+    fold_out_1,
+    fold_all_0,
+    fold_all_1,
     fold_at,
     load_sem,
-    out_sem,
     halo_send,
     halo_recv,
     pair_send,
@@ -88,6 +97,7 @@
     far = comp >= 2
     is_ocean = comp == 3
     folded = jnp.logical_and(is_ocean, lat == n_lat - 1)
+    fold_out, fold_all = (fold_out_0, fold_out_1), (fold_all_0, fold_all_1)
     sibling = (lon, lat, comp + 1 - 2 * core)
     partner = (lon, lat, lax.rem(comp + 2, 4))
 
@@ -123,9 +133,6 @@
         local(fields.at[0, pl.ds(1, SLICES - 1)], ext.at[pl.ds(2, SLICES - 1), MID_R, MID_C], 7),
     ]
     fold_load = local(fold.at[pl.ds(0, 1024)], fold_at, 8)
-    for load in loads:
-        load.start()
-
     barrier = pltpu.get_barrier_semaphore()
 
     def greet(target):
@@ -142,6 +149,9 @@
         for away in range(1, n_lon):
             greet((lax.rem(lon + away, n_lon), lat, comp))
 
+    for load in loads:
+        load.start()
+
     @pl.when(lat == 0)
     def _():
         ext[:, 0:PADR, :] = jnp.zeros((SLICES + 1, PADR, EXTC), F32)
@@ -150,6 +160,107 @@
     def _():
         ext[:, PADR + ROWS : EXTR, :] = jnp.zeros((SLICES + 1, PADR, EXTC), F32)
 
+    def halo(group, index):
+        east, north, src_r, src_c, dst_r, dst_c = SIDES[index]
+        way = 0 if north > 0 else 1
+        if group == 1 and index < 2:
+            src, dst = rows_out.at[way], rows_in.at[way]
+        elif group == 1 and index >= 4:
+            cells = pl.ds(COLS - PADC, PADC) if east > 0 else pl.ds(0, PADC)
+            src, dst = rows_out.at[way, pl.ds(8 - 8 * way, 8), cells], corner_in.at[index - 4]
+        elif group == 0 and index < 2:
+            src, dst = edge_out.at[way], ext.at[1, dst_r, dst_c]
+        elif group == 0 and index < 4:
+            src, dst = side_out.at[index - 2], ext.at[1, dst_r, dst_c]
+        else:
+            planes = pl.ds(2, SLICES - 1) if group == 1 else pl.ds(1, 1)
+            src, dst = ext.at[planes, src_r, src_c], ext.at[planes, dst_r, dst_c]
+        slot = group * N_SIDES + index
+        return pltpu.make_async_remote_copy(
+            src,
+            dst,
+            halo_send.at[slot],
+            halo_recv.at[slot],
+            device_id=side_target(east, north),
+            device_id_type=MESH,
+        )
+
+    def pack_surface():
+        line = lax.broadcasted_iota(jnp.int32, (PADR, COLS), 0)
+        for way, at, spare, turn in ((0, ROWS, 0, 1), (1, PADR, PADR - 1, -1)):
+            tile = ext[1, at : at + PADR, PADC : PADC + COLS]
+            rate = ext[0, at : at + PADR, PADC : PADC + COLS]
+            edge_out[way] = jnp.where(line == spare, roll(rate, turn, 0), tile)
+        lane = lax.broadcasted_iota(jnp.int32, (ROWS, PADC), 1)
+        for way, at, spare, turn in ((0, COLS, 0, 1), (1, PADC, PADC - 1, -1)):
+            tile = ext[1, PADR : PADR + ROWS, at : at + PADC]
+            rate = ext[0, PADR : PADR + ROWS, at : at + PADC]
+            side_out[way] = jnp.where(lane == spare, roll(rate, turn, 1), tile)
+
+    def unpack_surface():
+        @pl.when(lat > 0)
+        def _():
+            ext[0, :PADR, PADC : PADC + COLS] = roll(ext[1, :PADR, PADC : PADC + COLS], -1, 0)
+
+        @pl.when(lat < n_lat - 1)
+        def _():
+            beyond = slice(PADR + ROWS, EXTR)
+            ext[0, beyond, PADC : PADC + COLS] = roll(ext[1, beyond, PADC : PADC + COLS], 1, 0)
+
+        rows = slice(PADR, PADR + ROWS)
+        ext[0, rows, :PADC] = roll(ext[1, rows, :PADC], -1, 1)
+        ext[0, rows, PADC + COLS :] = roll(ext[1, rows, PADC + COLS :], 1, 1)
+
+    def pack_rows():
+        for plane in range(2, SLICES + 1):
+            at = plane - 2
+            tail = ext[plane, ROWS : ROWS + PADR, PADC : PADC + COLS]
+            head = ext[plane, PADR : 2 * PADR, PADC : PADC + COLS]
+            rows_out[0, at : at + 1, :] = tail[6:7]
+            rows_out[0, 8 + at : 9 + at, :] = tail[7:8]
+            rows_out[1, at : at + 1, :] = head[0:1]
+            rows_out[1, 8 + at : 9 + at, :] = head[1:2]
+        for way in range(2):
+            for at in (7, 15):
+                rows_out[way, at : at + 1, :] = jnp.zeros((1, COLS), F32)
+
+    def unpack_rows():
+        beyond = PADR + ROWS
+        sides = (slice(0, PADC), slice(PADC + COLS, EXTC))
+
+        @pl.when(lat > 0)
+        def _():
+            for plane in range(2, SLICES + 1):
+                at = plane - 2
+                ext[plane, PADR - 2 : PADR - 1, PADC : PADC + COLS] = rows_in[0, at : at + 1, :]
+                ext[plane, PADR - 1 : PADR, PADC : PADC + COLS] = rows_in[0, 8 + at : 9 + at, :]
+                for side in range(2):
+                    ext[plane, PADR - 1 : PADR, sides[side]] = corner_in[side, at : at + 1, :]
+
+        @pl.when(lat < n_lat - 1)
+        def _():
+            for plane in range(2, SLICES + 1):
+                at = plane - 2
+                ext[plane, beyond : beyond + 1, PADC : PADC + COLS] = rows_in[1, at : at + 1, :]
+                ext[plane, beyond + 1 : beyond + 2, PADC : PADC + COLS] = rows_in[1, 8 + at : 9 + at, :]
+                for side in range(2):
+                    ext[plane, beyond : beyond + 1, sides[side]] = corner_in[2 + side, at : at + 1, :]
+
+    def send_halos(group):
+        for index in reversed(range(N_SIDES)):
+            when(has(SIDES[index][1]), halo(group, index).start)
+
+    def await_halos(group):
+        for index in range(N_SIDES):
+            when(has(-SIDES[index][1]), halo(group, index).wait_recv)
+
+    def await_sent(group):
+        for index in range(N_SIDES):
+            when(has(SIDES[index][1]), halo(group, index).wait_send)
+
+    loads[0].wait()
+    loads[1].wait()
+    pack_surface()
     expected = (
         3
         + 3 * (lat > 0).astype(jnp.int32)
@@ -163,66 +274,61 @@
     def _():
         pl.semaphore_signal(ready, inc=1, device_id=partner, device_id_type=MESH)
 
-    def halo(group, index):
-        east, north, src_r, src_c, dst_r, dst_c = SIDES[index]
-        if group == 1:
-            planes = pl.ds(2, SLICES - 1)
-        elif index < 4:
-            planes = pl.ds(0, 2)
-        else:
-            planes = pl.ds(1, 1)
-        slot = group * N_SIDES + index
+    send_halos(0)
+
+    def fold_copy(group, away):
         return pltpu.make_async_remote_copy(
-            ext.at[planes, src_r, src_c],
-            ext.at[planes, dst_r, dst_c],
-            halo_send.at[slot],
-            halo_recv.at[slot],
-            device_id=side_target(east, north),
-            device_id_type=MESH,
-        )
-
-    def send_halos(group):
-        for index in range(N_SIDES):
-            when(has(SIDES[index][1]), halo(group, index).start)
-
-    def await_halos(group):
-        for index in range(N_SIDES):
-            when(has(-SIDES[index][1]), halo(group, index).wait_recv)
-
-    def await_sent(group):
-        for index in range(N_SIDES):
-            when(has(SIDES[index][1]), halo(group, index).wait_send)
-
-    loads[0].wait()
-    loads[1].wait()
-    send_halos(0)
-    loads[7].wait()
-    send_halos(1)
-
-    def fold_copy(away):
-        return pltpu.make_async_remote_copy(
-            fold_out,
-            fold_all.at[pl.ds(BLOCKS * lon, BLOCKS)],
-            fold_send.at[away],
-            fold_recv.at[away],
+            fold_out[group],
+            fold_all[group].at[pl.ds(BLOCKS * lon, BLOCKS)],
+            fold_send.at[group, away],
+            fold_recv.at[group, away],
             device_id=(lax.rem(lon + away, n_lon), lat, comp),
             device_id_type=MESH,
         )
 
+    def fold_pack(group):
+        for block in range(BLOCKS):
+            cols = slice(PADC + block * PADC, 2 * PADC + block * PADC)
+            for plane, at, row in FOLD_LINES[group]:
+                fold_out[group][block, at : at + 1, :] = ext[plane, PADR + row : PADR + row + 1, cols]
+        fold_all[group][pl.ds(BLOCKS * lon, BLOCKS)] = fold_out[group][...]
+        for away in range(1, n_lon):
+            fold_copy(group, away).start()
+
+    def fold_unpack(group):
+        for away in range(1, n_lon):
+            fold_copy(group, away).wait_recv()
+        ahead = fold_at[0] + n_lon * COLS - (lon + 1) * COLS
+        start = ahead // PADC
+        rest = lax.rem(ahead, PADC)
+        window = [fold_all[group][lax.rem(start + i, BLOCKS * n_lon)] for i in range(BLOCKS + 2)]
+        spots = lax.broadcasted_iota(jnp.int32, (2 * PADC, PADC), 0) + lax.broadcasted_iota(
+            jnp.int32, (2 * PADC, PADC), 1
+        )
+        pick = jnp.where(spots == PADC + rest, 1.0, 0.0).astype(F32)
+        for block in range(BLOCKS + 2):
+            pair = jnp.concatenate([window[max(BLOCKS - block, 0)], window[BLOCKS + 1 - block]], axis=1)
+            mirrored = jnp.dot(
+                pair, pick, precision=lax.Precision.HIGHEST, preferred_element_type=F32
+            )
+            cols = slice(block * PADC, (block + 1) * PADC)
+            for plane, at, row in FOLD_LINES[group]:
+                to = PADR + 2 * ROWS - 1 - row
+                ext[plane, to : to + 1, cols] = mirrored[at : at + 1]
+
     @pl.when(folded)
     def _():
-        fold_out[...] = jnp.zeros((BLOCKS, FOLD_ROWS, PADC), F32)
-        for block in range(BLOCKS):
-            at = PADC + block * PADC
-            for plane in range(SLICES):
-                tail = ext[plane + 1, ROWS : ROWS + PADR, at : at + PADC]
-                fold_out[block, plane : plane + 1, :] = tail[6:7]
-                fold_out[block, SLICES + plane : SLICES + plane + 1, :] = tail[7:8]
-            tail = ext[0, ROWS : ROWS + PADR, at : at + PADC]
-            fold_out[block, 2 * SLICES : 2 * SLICES + 1, :] = tail[7:8]
-        fold_all[pl.ds(BLOCKS * lon, BLOCKS)] = fold_out[...]
-        for away in range(1, n_lon):
-            fold_copy(away).start()
+        for packed in fold_out:
+            packed[...] = jnp.zeros(packed.shape, F32)
+        fold_pack(0)
+
+    loads[7].wait()
+    pack_rows()
+    send_halos(1)
+
+    @pl.when(folded)
+    def _():
+        fold_pack(1)
 
     loads[2].wait()
     loads[3].wait()
@@ -248,34 +354,6 @@
             return carry
 
         lax.fori_loop(0, ROWS // 8, rows_of, 0)
-
-    @pl.when(folded)
-    def _():
-        for away in range(1, n_lon):
-            fold_copy(away).wait_recv()
-        fold_load.wait()
-        ahead = fold_at[0] + n_lon * COLS - (lon + 1) * COLS
-        start = ahead // PADC
-        rest = lax.rem(ahead, PADC)
-        total = BLOCKS * n_lon
-        window = [fold_all[lax.rem(start + i, total)] for i in range(BLOCKS + 2)]
-        spots = lax.broadcasted_iota(jnp.int32, (2 * PADC, PADC), 0) + lax.broadcasted_iota(
-            jnp.int32, (2 * PADC, PADC), 1
-        )
-        pick = jnp.where(spots == PADC + rest, 1.0, 0.0).astype(F32)
-        for block in range(BLOCKS + 2):
-            pair = jnp.concatenate([window[max(BLOCKS - block, 0)], window[BLOCKS + 1 - block]], axis=1)
-            mirrored = jnp.dot(
-                pair, pick, precision=lax.Precision.HIGHEST, preferred_element_type=F32
-            )
-            cols = slice(block * PADC, (block + 1) * PADC)
-            beyond = PADR + ROWS
-            for plane in range(SLICES):
-                ext[plane + 1, beyond + 1 : beyond + 2, cols] = mirrored[plane : plane + 1]
-                ext[plane + 1, beyond : beyond + 1, cols] = mirrored[
-                    SLICES + plane : SLICES + plane + 1
-                ]
-            ext[0, beyond : beyond + 1, cols] = mirrored[2 * SLICES : 2 * SLICES + 1]
 
     def first_substep(plane):
         for block in range(EXTR // 8):
@@ -305,6 +383,13 @@
         return here + rate * (north + south + east + west - 4.0 * here)
 
     await_halos(0)
+    unpack_surface()
+
+    @pl.when(folded)
+    def _():
+        fold_load.wait()
+        fold_unpack(0)
+
     first_substep(1)
 
     @pl.when(is_ocean)
@@ -322,7 +407,7 @@
             lowest = second_substep(1, block)
             flux = exch[rows, :] * (seen[rows, :].astype(F32) - lowest)
             flux = flux.astype(BF16).astype(F32)
-            upd[0, rows, :] = lowest + AIR_GAIN * flux
+            updated[0, 0, rows, :] = lowest + AIR_GAIN * flux
             at = PADR + block * 8
             padded[at : at + 8, PADC : PADC + COLS] = flux
             padded[at : at + 8, :PADC] = jnp.broadcast_to(flux[:, :1], (8, PADC))
@@ -362,31 +447,29 @@
     pl.when(far)(cross.start)
 
     await_halos(1)
+    unpack_rows()
+
+    @pl.when(folded)
+    def _():
+        fold_unpack(1)
 
     def other_slice(plane, carry):
         first_substep(plane)
         for block in range(ROWS // 8):
-            upd[plane - 1, block * 8 : block * 8 + 8, :] = second_substep(plane, block)
+            updated[0, plane - 1, block * 8 : block * 8 + 8, :] = second_substep(plane, block)
         return carry
 
     lax.fori_loop(2, SLICES + 1, other_slice, 0)
-    rest_out = pltpu.make_async_copy(
-        upd.at[pl.ds(1, SLICES - 1)], updated.at[0, pl.ds(1, SLICES - 1)], out_sem.at[0]
-    )
-    top_out = pltpu.make_async_copy(upd.at[0], updated.at[0, 0], out_sem.at[1])
-    con_out = pltpu.make_async_copy(con, contrast.at[0], out_sem.at[2])
-    rest_out.start()
 
     @pl.when(jnp.logical_not(far))
     def _():
         pl.semaphore_wait(ready, 1)
         cross.start()
-
-    pl.when(jnp.logical_not(is_ocean))(top_out.start)
 
     cross.wait_recv()
     surf[core] = part[...] + part_in[...]
     finish.start()
+
     finish.wait_recv()
 
     for block in range(ROWS // 8):
@@ -396,15 +479,12 @@
 
         @pl.when(is_ocean)
         def _():
-            upd[0, rows, :] = ocean
-            con[rows, :] = sea_new - seen[rows, :].astype(F32)
+            updated[0, 0, rows, :] = ocean
+            contrast[0, rows, :] = sea_new - seen[rows, :].astype(F32)
 
         @pl.when(jnp.logical_not(is_ocean))
         def _():
-            con[rows, :] = sea_new - upd[0, rows, :]
-
-    con_out.start()
-    pl.when(is_ocean)(top_out.start)
+            contrast[0, rows, :] = sea_new - updated[0, 0, rows, :]
 
     await_sent(0)
     await_sent(1)
@@ -415,11 +495,8 @@
     @pl.when(folded)
     def _():
         for away in range(1, n_lon):
-            fold_copy(away).wait_send()
-
-    rest_out.wait()
-    top_out.wait()
-    con_out.wait()
+            fold_copy(0, away).wait_send()
+            fold_copy(1, away).wait_send()
 
 
 def shards(n_lon, n_lat, *args):
@@ -428,16 +505,14 @@
     return pl.pallas_call(
         functools.partial(kernel, n_lon, n_lat),
         out_shape=(
-            jax.ShapeDtypeStruct(fields.shape, F32),
-            jax.ShapeDtypeStruct((1, ROWS, COLS), F32),
+            pltpu.VMEM(fields.shape, F32),
+            pltpu.VMEM((1, ROWS, COLS), F32),
         ),
         in_specs=[pl.BlockSpec(memory_space=pl.ANY)] * 8,
-        out_specs=(pl.BlockSpec(memory_space=pl.ANY),) * 2,
+        out_specs=(pl.BlockSpec(memory_space=pltpu.VMEM),) * 2,
         scratch_shapes=[
             vmem((SLICES + 1, EXTR, EXTC), F32),
             vmem((SLICES, EXTR, EXTC), F32),
-            vmem((SLICES, ROWS, COLS), F32),
-            vmem((ROWS, COLS), F32),
             vmem((ROWS, COLS), F32),
             vmem((ROWS, COLS), BF16),
             vmem((TAPS, ROWS, COLS), jnp.int32),
@@ -451,23 +526,29 @@
             vmem((ROWS, HALF), F32),
             vmem((ROWS, HALF), F32),
             vmem((2, ROWS, HALF), F32),
-            vmem((BLOCKS, FOLD_ROWS, PADC), F32),
-            vmem((BLOCKS * n_lon, FOLD_ROWS, PADC), F32),
+            vmem((2, PADR, COLS), F32),
+            vmem((2, ROWS, PADC), F32),
+            vmem((2, 16, COLS), F32),
+            vmem((2, 16, COLS), F32),
+            vmem((4, 8, PADC), F32),
+            vmem((BLOCKS, 8, PADC), F32),
+            vmem((BLOCKS, 16, PADC), F32),
+            vmem((BLOCKS * n_lon, 8, PADC), F32),
+            vmem((BLOCKS * n_lon, 16, PADC), F32),
             pltpu.SMEM((1024,), jnp.int32),
             sems((9,)),
-            sems((3,)),
             sems((2 * N_SIDES,)),
             sems((2 * N_SIDES,)),
             sems((3,)),
             sems((3,)),
-            sems((n_lon,)),
-            sems((n_lon,)),
+            sems((2, n_lon)),
+            sems((2, n_lon)),
             pltpu.SemaphoreType.REGULAR,
         ],
         compiler_params=pltpu.CompilerParams(
             collective_id=0, has_side_effects=True, vmem_limit_bytes=32 * 2**20
         ),
-    )(*args)
+    )(*[pltpu.with_memory_space_constraint(a, pltpu.HBM) for a in args])
 
 
 def solution(mesh):

time: 54.9 us -> 45.6 us (0.83)
  the two profiles are of different devices: /device:TPU:481 before, /device:TPU:105 now
where the time goes in v2:
time: 45.6 us; the launch traced here: 45.5 us
  Pallas kernels  43.3 us (95%)
  local copies, waits for them, and re-layouts  1.52 us (3%)
  between operations  0.64 us (1%)
    pallas_call x1, Pallas kernels, shards(): pl.pallas_call(functools.partial(kernel, n_lon, n_lat), out_shape=(pltpu....  43.3 us
    unnamed x2, local copies, waits for them, and re-layouts  1.52 us

profile of v2, /device:TPU:105, one launch (start us, length us, event | category | flops | bytes accessed | tf_op | source)
XLA Modules:
  0.0 45.5 jit_solution(13597338672458616404)
XLA Ops:
  0.6 43.3 %shard_map.95 = (f32[1,8,48,512]{3,2,1,0:T(8,128)S(1)}, f32[1,48,512]{2,1,0:T(8,128)S(1)}) custom-call(f32[1,8,48,512]{3,2,1,0:T(8,128)} %fields.1, f32[1,48,512]{2,1,0:T(8,128)} %diffusion.1, f32[1,48,512]{2,1,0:T(8,128)} %exchange.1, bf16[48,512]{1,0:T(8,128)(2,1)} %sea_seen.1, s32[8,48,512]{2,1,0:T(8,128)} %code.1, f32[8,48,512]{2,1,0:T(8,128)} %weight.1, ...), custom_call_target="tpu_custom_call" | custom-call | tf_op jit(solution)/shard_map/pallas_call | solution.py:505
  43.9 0.9 %copy.12 = f32[1,8,48,512]{3,2,1,0:T(8,128)} copy(f32[1,8,48,512]{3,2,1,0:T(8,128)S(1)} %get-tuple-element.2) | data formatting | bytes 1572864
  44.8 0.6 %copy.13 = f32[1,48,512]{2,1,0:T(8,128)} copy(f32[1,48,512]{2,1,0:T(8,128)S(1)} %get-tuple-element.3) | data formatting | bytes 196608

commit v3 on v2

--- a/solution.py
+++ b/solution.py
@@ -499,10 +499,21 @@
             fold_copy(1, away).wait_send()
 
 
+def store(updated, contrast, updated_out, contrast_out, sem):
+    copies = [
+        pltpu.make_async_copy(contrast, contrast_out, sem.at[0]),
+        pltpu.make_async_copy(updated, updated_out, sem.at[1]),
+    ]
+    for copy in copies:
+        copy.start()
+    for copy in copies:
+        copy.wait()
+
+
 def shards(n_lon, n_lat, *args):
     fields = args[0]
     vmem, sems = pltpu.VMEM, pltpu.SemaphoreType.DMA
-    return pl.pallas_call(
+    results = pl.pallas_call(
         functools.partial(kernel, n_lon, n_lat),
         out_shape=(
             pltpu.VMEM(fields.shape, F32),
@@ -549,6 +560,13 @@
             collective_id=0, has_side_effects=True, vmem_limit_bytes=32 * 2**20
         ),
     )(*[pltpu.with_memory_space_constraint(a, pltpu.HBM) for a in args])
+    return pl.pallas_call(
+        store,
+        out_shape=tuple(jax.ShapeDtypeStruct(r.shape, r.dtype) for r in results),
+        in_specs=[pl.BlockSpec(memory_space=pltpu.VMEM)] * 2,
+        out_specs=(pl.BlockSpec(memory_space=pl.ANY),) * 2,
+        scratch_shapes=[sems((2,))],
+    )(*[pltpu.with_memory_space_constraint(r, pltpu.VMEM) for r in results])
 
 
 def solution(mesh):

time: 45.6 us -> 45.1 us (0.989)
  local copies, waits for them, and re-layouts: 1.52 us -> 0 us
  Pallas kernels: 43.3 us -> 44.2 us
    unnamed x2 -> x0, local copies, waits for them, and re-layouts: 1.52 us -> none
    pallas_call x0 -> x1, Pallas kernels: none -> 0.93 us  [shards(): pl.pallas_call(store, out_shape=tuple((jax.ShapeDtypeStruct(r.shape, r.dt...]
where the time goes in v3:
time: 45.1 us; the launch traced here: 44.9 us
  Pallas kernels  44.2 us (98%)
  between operations  0.64 us (1%)
    pallas_call x1, Pallas kernels, shards(): pl.pallas_call(functools.partial(kernel, n_lon, n_lat), out_shape=(pltpu....  43.3 us
    pallas_call x1, Pallas kernels, shards(): pl.pallas_call(store, out_shape=tuple((jax.ShapeDtypeStruct(r.shape, r.dt...  0.93 us

profile of v3, /device:TPU:105, one launch (start us, length us, event | category | flops | bytes accessed | tf_op | source)
XLA Modules:
  0.0 44.9 jit_solution(17570733030915932466)
XLA Ops:
  0.6 43.3 %shard_map.95 = (f32[1,8,48,512]{3,2,1,0:T(8,128)S(1)}, f32[1,48,512]{2,1,0:T(8,128)S(1)}) custom-call(f32[1,8,48,512]{3,2,1,0:T(8,128)} %fields.1, f32[1,48,512]{2,1,0:T(8,128)} %diffusion.1, f32[1,48,512]{2,1,0:T(8,128)} %exchange.1, bf16[48,512]{1,0:T(8,128)(2,1)} %sea_seen.1, s32[8,48,512]{2,1,0:T(8,128)} %code.1, f32[8,48,512]{2,1,0:T(8,128)} %weight.1, ...), custom_call_target="tpu_custom_call" | custom-call | tf_op jit(solution)/shard_map/pallas_call | solution.py:516
  43.9 0.9 %shard_map.96 = (f32[1,8,48,512]{3,2,1,0:T(8,128)}, f32[1,48,512]{2,1,0:T(8,128)}) custom-call(f32[1,8,48,512]{3,2,1,0:T(8,128)S(1)} %get-tuple-element.4.updated, f32[1,48,512]{2,1,0:T(8,128)S(1)} %get-tuple-element.5.contrast), custom_call_target="tpu_custom_call" | custom-call | tf_op jit(solution)/shard_map/pallas_call | solution.py:563

commit v4 on v3

--- a/solution.py
+++ b/solution.py
@@ -62,6 +62,7 @@
     mid,
     exch,
     seen,
+    prior,
     codes,
     weights,
     sea_mask,
@@ -335,6 +336,8 @@
     loads[4].wait()
     loads[5].wait()
     loads[6].wait()
+    for at in range(0, ROWS, 16):
+        prior[at : at + 16, :] = seen[at : at + 16, :].astype(F32)
 
     @pl.when(jnp.logical_not(is_ocean))
     def _():
@@ -405,7 +408,7 @@
         for block in range(ROWS // 8):
             rows = slice(block * 8, block * 8 + 8)
             lowest = second_substep(1, block)
-            flux = exch[rows, :] * (seen[rows, :].astype(F32) - lowest)
+            flux = exch[rows, :] * (prior[rows, :] - lowest)
             flux = flux.astype(BF16).astype(F32)
             updated[0, 0, rows, :] = lowest + AIR_GAIN * flux
             at = PADR + block * 8
@@ -480,7 +483,7 @@
         @pl.when(is_ocean)
         def _():
             updated[0, 0, rows, :] = ocean
-            contrast[0, rows, :] = sea_new - seen[rows, :].astype(F32)
+            contrast[0, rows, :] = sea_new - prior[rows, :]
 
         @pl.when(jnp.logical_not(is_ocean))
         def _():
@@ -526,6 +529,7 @@
             vmem((SLICES, EXTR, EXTC), F32),
             vmem((ROWS, COLS), F32),
             vmem((ROWS, COLS), BF16),
+            vmem((ROWS, COLS), F32),
             vmem((TAPS, ROWS, COLS), jnp.int32),
             vmem((TAPS, ROWS, COLS), F32),
             vmem((ROWS, COLS), jnp.int32),

time: 45.1 us -> 45.1 us (level)
  no operation moved by 1% of the time
where the time goes in v4:
time: 45.1 us; the launch traced here: 44.9 us
  Pallas kernels  44.2 us (98%)
  between operations  0.64 us (1%)
    pallas_call x1, Pallas kernels, shards(): pl.pallas_call(functools.partial(kernel, n_lon, n_lat), out_shape=(pltpu....  43.3 us
    pallas_call x1, Pallas kernels, shards(): pl.pallas_call(store, out_shape=tuple((jax.ShapeDtypeStruct(r.shape, r.dt...  0.93 us

profile of v4, /device:TPU:105, one launch (start us, length us, event | category | flops | bytes accessed | tf_op | source)
XLA Modules:
  0.0 44.9 jit_solution(4755672217496362994)
XLA Ops:
  0.6 43.3 %shard_map.95 = (f32[1,8,48,512]{3,2,1,0:T(8,128)S(1)}, f32[1,48,512]{2,1,0:T(8,128)S(1)}) custom-call(f32[1,8,48,512]{3,2,1,0:T(8,128)} %fields.1, f32[1,48,512]{2,1,0:T(8,128)} %diffusion.1, f32[1,48,512]{2,1,0:T(8,128)} %exchange.1, bf16[48,512]{1,0:T(8,128)(2,1)} %sea_seen.1, s32[8,48,512]{2,1,0:T(8,128)} %code.1, f32[8,48,512]{2,1,0:T(8,128)} %weight.1, ...), custom_call_target="tpu_custom_call" | custom-call | tf_op jit(solution)/shard_map/pallas_call | solution.py:519
  43.9 0.9 %shard_map.96 = (f32[1,8,48,512]{3,2,1,0:T(8,128)}, f32[1,48,512]{2,1,0:T(8,128)}) custom-call(f32[1,8,48,512]{3,2,1,0:T(8,128)S(1)} %get-tuple-element.4.updated, f32[1,48,512]{2,1,0:T(8,128)S(1)} %get-tuple-element.5.contrast), custom_call_target="tpu_custom_call" | custom-call | tf_op jit(solution)/shard_map/pallas_call | solution.py:567

commit v5 on v4

--- a/solution.py
+++ b/solution.py
@@ -13,6 +13,7 @@
 PADR, PADC = 8, 128
 EXTR, EXTC = ROWS + 2 * PADR, COLS + 2 * PADC
 HALF = COLS // 2
+CHUNKS = (pl.ds(0, 32), pl.ds(32, 16))
 BLOCKS = COLS // PADC
 N_SIDES = 8
 AIR_GAIN = 0.5
@@ -134,12 +135,15 @@
         local(fields.at[0, pl.ds(1, SLICES - 1)], ext.at[pl.ds(2, SLICES - 1), MID_R, MID_C], 7),
     ]
     fold_load = local(fold.at[pl.ds(0, 1024)], fold_at, 8)
+    loads[0].start()
+    loads[1].start()
+
     barrier = pltpu.get_barrier_semaphore()
 
     def greet(target):
         pl.semaphore_signal(barrier, inc=1, device_id=target, device_id_type=MESH)
 
-    for east, north, *_ in SIDES:
+    for east, north, *_ in reversed(SIDES):
         when(has(north), functools.partial(greet, side_target(east, north)))
     greet(sibling)
     pl.when(jnp.logical_not(far))(functools.partial(greet, partner))
@@ -150,7 +154,7 @@
         for away in range(1, n_lon):
             greet((lax.rem(lon + away, n_lon), lat, comp))
 
-    for load in loads:
+    for load in loads[2:]:
         load.start()
 
     @pl.when(lat == 0)
@@ -169,13 +173,16 @@
         elif group == 1 and index >= 4:
             cells = pl.ds(COLS - PADC, PADC) if east > 0 else pl.ds(0, PADC)
             src, dst = rows_out.at[way, pl.ds(8 - 8 * way, 8), cells], corner_in.at[index - 4]
+        elif group == 0 and index >= 4:
+            rows = pl.ds(ROWS - PADR, PADR) if north > 0 else pl.ds(0, PADR)
+            cols = pl.ds(COLS - PADC, PADC) if east > 0 else pl.ds(0, PADC)
+            src, dst = fields.at[0, 0, rows, cols], ext.at[1, dst_r, dst_c]
         elif group == 0 and index < 2:
             src, dst = edge_out.at[way], ext.at[1, dst_r, dst_c]
         elif group == 0 and index < 4:
             src, dst = side_out.at[index - 2], ext.at[1, dst_r, dst_c]
         else:
-            planes = pl.ds(2, SLICES - 1) if group == 1 else pl.ds(1, 1)
-            src, dst = ext.at[planes, src_r, src_c], ext.at[planes, dst_r, dst_c]
+            src, dst = ext.at[pl.ds(2, SLICES - 1), src_r, src_c], ext.at[pl.ds(2, SLICES - 1), dst_r, dst_c]
         slot = group * N_SIDES + index
         return pltpu.make_async_remote_copy(
             src,
@@ -247,8 +254,8 @@
                 for side in range(2):
                     ext[plane, beyond : beyond + 1, sides[side]] = corner_in[2 + side, at : at + 1, :]
 
-    def send_halos(group):
-        for index in reversed(range(N_SIDES)):
+    def send_halos(group, order):
+        for index in order:
             when(has(SIDES[index][1]), halo(group, index).start)
 
     def await_halos(group):
@@ -259,9 +266,6 @@
         for index in range(N_SIDES):
             when(has(SIDES[index][1]), halo(group, index).wait_send)
 
-    loads[0].wait()
-    loads[1].wait()
-    pack_surface()
     expected = (
         3
         + 3 * (lat > 0).astype(jnp.int32)
@@ -275,7 +279,11 @@
     def _():
         pl.semaphore_signal(ready, inc=1, device_id=partner, device_id_type=MESH)
 
-    send_halos(0)
+    send_halos(0, range(4, N_SIDES))
+    loads[0].wait()
+    loads[1].wait()
+    pack_surface()
+    send_halos(0, (2, 3, 0, 1))
 
     def fold_copy(group, away):
         return pltpu.make_async_remote_copy(
@@ -325,7 +333,7 @@
 
     loads[7].wait()
     pack_rows()
-    send_halos(1)
+    send_halos(1, range(N_SIDES))
 
     @pl.when(folded)
     def _():
@@ -441,13 +449,18 @@
         )
 
     give = pair_copy(0, share.at[1 - core], share_in, sibling)
-    cross = pair_copy(1, part, part_in, partner)
-    finish = pair_copy(2, surf.at[core], surf.at[core], sibling)
+    cross = [pair_copy(1 + i, part.at[c], part_in.at[c], partner) for i, c in enumerate(CHUNKS)]
+    finish = [pair_copy(3 + i, surf.at[core, c], surf.at[core, c], sibling) for i, c in enumerate(CHUNKS)]
+
+    def start_cross():
+        for piece in cross:
+            piece.start()
+
     give.start()
     give.wait_recv()
     part[...] = share[core] + share_in[...]
 
-    pl.when(far)(cross.start)
+    pl.when(far)(start_cross)
 
     await_halos(1)
     unpack_rows()
@@ -467,33 +480,34 @@
     @pl.when(jnp.logical_not(far))
     def _():
         pl.semaphore_wait(ready, 1)
-        cross.start()
-
-    cross.wait_recv()
-    surf[core] = part[...] + part_in[...]
-    finish.start()
-
-    finish.wait_recv()
-
-    for block in range(ROWS // 8):
-        rows = slice(block * 8, block * 8 + 8)
-        ocean = jnp.concatenate([surf[0, rows, :], surf[1, rows, :]], axis=1)
-        sea_new = ocean.astype(BF16).astype(F32)
-
-        @pl.when(is_ocean)
-        def _():
-            updated[0, 0, rows, :] = ocean
-            contrast[0, rows, :] = sea_new - prior[rows, :]
-
-        @pl.when(jnp.logical_not(is_ocean))
-        def _():
-            contrast[0, rows, :] = sea_new - updated[0, 0, rows, :]
+        start_cross()
+
+    for piece, chunk in enumerate(CHUNKS):
+        cross[piece].wait_recv()
+        surf[core, chunk] = part[chunk] + part_in[chunk]
+        finish[piece].start()
+
+    for piece, chunk in enumerate(CHUNKS):
+        finish[piece].wait_recv()
+        for at in range(chunk.start, chunk.start + chunk.size, 8):
+            rows = slice(at, at + 8)
+            ocean = jnp.concatenate([surf[0, rows, :], surf[1, rows, :]], axis=1)
+            sea_new = ocean.astype(BF16).astype(F32)
+
+            @pl.when(is_ocean)
+            def _():
+                updated[0, 0, rows, :] = ocean
+                contrast[0, rows, :] = sea_new - prior[rows, :]
+
+            @pl.when(jnp.logical_not(is_ocean))
+            def _():
+                contrast[0, rows, :] = sea_new - updated[0, 0, rows, :]
 
     await_sent(0)
     await_sent(1)
     give.wait_send()
-    cross.wait_send()
-    finish.wait_send()
+    for piece in cross + finish:
+        piece.wait_send()
 
     @pl.when(folded)
     def _():
@@ -554,8 +568,8 @@
             sems((9,)),
             sems((2 * N_SIDES,)),
             sems((2 * N_SIDES,)),
-            sems((3,)),
-            sems((3,)),
+            sems((5,)),
+            sems((5,)),
             sems((2, n_lon)),
             sems((2, n_lon)),
             pltpu.SemaphoreType.REGULAR,

time: 45.1 us -> 45.1 us (level)
  no operation moved by 1% of the time
where the time goes in v5:
time: 45.1 us; the launch traced here: 44.9 us
  Pallas kernels  44.3 us (98%)
  between operations  0.64 us (1%)
    pallas_call x1, Pallas kernels, shards(): pl.pallas_call(functools.partial(kernel, n_lon, n_lat), out_shape=(pltpu....  43.4 us
    pallas_call x1, Pallas kernels, shards(): pl.pallas_call(store, out_shape=tuple((jax.ShapeDtypeStruct(r.shape, r.dt...  0.93 us

profile of v5, /device:TPU:105, one launch (start us, length us, event | category | flops | bytes accessed | tf_op | source)
XLA Modules:
  0.0 44.9 jit_solution(1196546460314741495)
XLA Ops:
  0.6 43.4 %shard_map.95 = (f32[1,8,48,512]{3,2,1,0:T(8,128)S(1)}, f32[1,48,512]{2,1,0:T(8,128)S(1)}) custom-call(f32[1,8,48,512]{3,2,1,0:T(8,128)} %fields.1, f32[1,48,512]{2,1,0:T(8,128)} %diffusion.1, f32[1,48,512]{2,1,0:T(8,128)} %exchange.1, bf16[48,512]{1,0:T(8,128)(2,1)} %sea_seen.1, s32[8,48,512]{2,1,0:T(8,128)} %code.1, f32[8,48,512]{2,1,0:T(8,128)} %weight.1, ...), custom_call_target="tpu_custom_call" | custom-call | tf_op jit(solution)/shard_map/pallas_call | solution.py:533
  44.0 0.9 %shard_map.96 = (f32[1,8,48,512]{3,2,1,0:T(8,128)}, f32[1,48,512]{2,1,0:T(8,128)}) custom-call(f32[1,8,48,512]{3,2,1,0:T(8,128)S(1)} %get-tuple-element.4.updated, f32[1,48,512]{2,1,0:T(8,128)S(1)} %get-tuple-element.5.contrast), custom_call_target="tpu_custom_call" | custom-call | tf_op jit(solution)/shard_map/pallas_call | solution.py:581
